TPU v7x, 512 devices: a whole 4x4x16 slice. The times are simulated.
512 devices in a mesh: lat: 128 (over y, z, core), ch: 4 (over x).
Axes of the slice: x: 4, y: 4, z: 16, core: 2. Of those that a mesh axis runs over, the one named last changes fastest.
Arguments:
- features: bfloat16 [128, 512, 1440], P('ch', 'lat'), may hold values from -6 to 6
- projection: float32 [128, 512], replicated, may hold values from -0.25 to 0.25
- synthesis: float32 [512, 128], replicated, may hold values from -0.5 to 0.5
- mode_weights: bfloat16 [128, 2, 128, 128], P('lat'), may hold values from -0.375 to 0.375
- skip_weights: bfloat16 [128, 128], replicated, may hold values from -0.5 to 0.5
- cotangent: bfloat16 [128, 512, 1440], P('ch', 'lat'), may hold values from -6 to 6
Outputs:
- output: bfloat16 [128, 512, 1440], P('ch', 'lat')
- grad_features: bfloat16 [128, 512, 1440], P('ch', 'lat')
- grad_weights: float32 [128, 2, 128, 128], P('lat', None, None, 'ch')
- grad_skip: float32 [128, 128], P(None, 'ch')
All inputs are finite; a program needn't handle non-finite values.
Results may differ from a plain program's by a relative error of at most 0.018.
Values may be sent and summed in bfloat16 or wider, within the bound.
A program may use at most 64 MiB of HBM per device.

v0:
```python
import math

import jax
import jax.numpy as jnp
from jax import lax
from jax.sharding import PartitionSpec as P

M = 64


def build_tables(length, mode_count):
    column = jnp.arange(length, dtype=jnp.int32)
    mode_index = jnp.arange(mode_count, dtype=jnp.int32)
    phase_turns = column[:, None] * mode_index[None, :] % length
    phases = phase_turns.astype(jnp.float32) * (2.0 * math.pi / length)
    factor = 1.0 / math.sqrt(length)
    doubling = jnp.where(mode_index == 0, 1.0, 2.0).astype(jnp.float32)
    forward_table = (jnp.concatenate([jnp.cos(phases), -jnp.sin(phases)], 1) * factor).astype(
        jnp.bfloat16
    )
    inverse_table = (
        jnp.concatenate([jnp.cos(phases) * doubling, -jnp.sin(phases) * doubling], 1) * factor
    ).T.astype(jnp.bfloat16)
    return (forward_table, inverse_table)


def product(form, left, right):
    return jnp.einsum(form, left, right, preferred_element_type=jnp.float32)


def project_modes(values, matrix, band_rows):
    start_row = lax.axis_index("lat") * band_rows
    columns = lax.dynamic_slice_in_dim(matrix, start_row, band_rows, 1)
    return lax.psum_scatter(
        jnp.dot(
            columns, values, precision=lax.Precision.HIGHEST, preferred_element_type=jnp.float32
        ),
        "lat",
        scatter_dimension=0,
        tiled=True,
    )


def gather_modes(coefficients, row_matrix):
    return jnp.dot(
        row_matrix,
        lax.all_gather(coefficients, "lat", axis=0, tiled=True).astype(jnp.float32),
        precision=lax.Precision.HIGHEST,
        preferred_element_type=jnp.float32,
    )


def on_device(features, projection, synthesis, mode_weights, skip_weights, cotangent):
    channels_dev, band_rows, length = features.shape
    owned_modes = mode_weights.shape[0]
    item_count = channels_dev * 2 * M
    forward_table, inverse_table = build_tables(length, M)
    lat_start = lax.axis_index("lat") * band_rows
    channel_start = lax.axis_index("ch") * channels_dev
    x_modes = product("cln,nj->lcj", features, forward_table).reshape(band_rows, item_count)
    spectral = (
        project_modes(x_modes, projection, band_rows)
        .astype(jnp.bfloat16)
        .reshape(owned_modes, channels_dev, 2 * M)
    )
    spectral_all = lax.all_gather(spectral, "ch", axis=1, tiled=True)
    weight_cols = lax.dynamic_slice_in_dim(mode_weights, channel_start, channels_dev, 3)
    w_real = weight_cols[:, 0]
    w_imag = weight_cols[:, 1]
    s_real = spectral_all[:, :, :M]
    s_imag = spectral_all[:, :, M:]
    out_real = product("lco,lcm->lom", w_real, s_real) - product("lco,lcm->lom", w_imag, s_imag)
    out_imag = product("lco,lcm->lom", w_real, s_imag) + product("lco,lcm->lom", w_imag, s_real)
    mixed = (
        jnp.concatenate([out_real, out_imag], 2)
        .astype(jnp.bfloat16)
        .reshape(owned_modes, item_count)
    )
    synthesis_rows = lax.dynamic_slice_in_dim(synthesis, lat_start, band_rows, 0)
    v_modes = (
        gather_modes(mixed, synthesis_rows)
        .astype(jnp.bfloat16)
        .reshape(band_rows, channels_dev, 2 * M)
    )
    spectral_field = product("lcj,jn->cln", v_modes, inverse_table)
    features_all = lax.all_gather(features, "ch", axis=0, tiled=True)
    skip_cols = lax.dynamic_slice_in_dim(skip_weights, channel_start, channels_dev, 1)
    skip_field = product("co,cln->oln", skip_cols, features_all)
    activation_in = spectral_field + skip_field
    output_field, pullback = jax.vjp(jax.nn.gelu, activation_in)
    g_pre = pullback(cotangent.astype(jnp.float32))[0].astype(jnp.bfloat16)
    g_vmodes = product("oln,jn->loj", g_pre, inverse_table).reshape(band_rows, item_count)
    g_mixed = (
        project_modes(g_vmodes, synthesis.T, band_rows)
        .astype(jnp.bfloat16)
        .reshape(owned_modes, channels_dev, 2 * M)
    )
    g_mixed_all = lax.all_gather(g_mixed, "ch", axis=1, tiled=True)
    weight_rows = lax.dynamic_slice_in_dim(mode_weights, channel_start, channels_dev, 2)
    r_real = weight_rows[:, 0]
    r_imag = weight_rows[:, 1]
    all_real = g_mixed_all[:, :, :M]
    all_imag = g_mixed_all[:, :, M:]
    back_real = product("lco,lom->lcm", r_real, all_real) + product(
        "lco,lom->lcm", r_imag, all_imag
    )
    back_imag = product("lco,lom->lcm", r_real, all_imag) - product(
        "lco,lom->lcm", r_imag, all_real
    )
    g_spectral = (
        jnp.concatenate([back_real, back_imag], 2)
        .astype(jnp.bfloat16)
        .reshape(owned_modes, item_count)
    )
    own_real = g_mixed[:, :, :M]
    own_imag = g_mixed[:, :, M:]
    grad_zero = product("lcm,lom->lco", s_real, own_real) + product(
        "lcm,lom->lco", s_imag, own_imag
    )
    grad_one = product("lcm,lom->lco", s_real, own_imag) - product("lcm,lom->lco", s_imag, own_real)
    grad_weights = jnp.stack([grad_zero, grad_one], 1) / math.sqrt(2 * M)
    projection_cols = lax.dynamic_slice_in_dim(projection, lat_start, band_rows, 1)
    g_xmodes = (
        gather_modes(g_spectral, projection_cols.T)
        .astype(jnp.bfloat16)
        .reshape(band_rows, channels_dev, 2 * M)
    )
    g_spectral_field = product("lcj,nj->cln", g_xmodes, forward_table)
    g_pre_all = lax.all_gather(g_pre, "ch", axis=0, tiled=True)
    skip_rows = lax.dynamic_slice_in_dim(skip_weights, channel_start, channels_dev, 0)
    g_skip = product("co,oln->cln", skip_rows, g_pre_all)
    grad_features = (g_spectral_field + g_skip).astype(jnp.bfloat16)
    skip_partial = product("cln,oln->co", features_all, g_pre)
    total_points = band_rows * lax.axis_size("lat") * length
    grad_skip = lax.psum(skip_partial, "lat") / math.sqrt(total_points)
    return (output_field.astype(jnp.bfloat16), grad_features, grad_weights, grad_skip)


def solution(mesh):
    placed = (P("ch", "lat", None), P(), P(), P("lat", None, None, None), P(), P("ch", "lat", None))
    return jax.shard_map(
        on_device,
        mesh=mesh,
        in_specs=placed,
        out_specs=(
            P("ch", "lat", None),
            P("ch", "lat", None),
            P("lat", None, None, "ch"),
            P(None, "ch"),
        ),
        check_vma=False,
    )
```

profile of v0, /device:TPU:1, one launch (start us, length us, event | category | flops | bytes accessed | tf_op | source)
XLA Modules:
  0.0 1423.9 jit_solution(8076043131791089138)
XLA Ops:
  7.2 3.1 sine_negate_fusion
  10.3 0.3 fusion.35
  10.6 0.3 convolution_bitcast_fusion.3
  10.9 2.7 fusion.40
  13.6 516.1 %all-reduce.5 = bf16[128,4096]{1,0:T(8,128)(2,1)} all-reduce(f32[128,4096]{1,0:T(8,128)S(1)} %fusion.40), channel_id=2, replica_groups=mesh['lat'=128,'ch'=4] {'lat'}, use_global_device_ids=true, to_apply=%region_0.1.clone | all-reduce | flops 524288 | bytes 3145728
  529.7 1.3 dynamic-slice.1
  531.0 1.5 fusion.58
  532.5 9.4 all_gather.18
  541.9 0.2 fusion.53
  542.1 0.2 fusion.54
  542.4 0.3 fusion.11
  542.6 0.3 fusion.12
  543.0 0.6 reshape.201
  543.7 0.8 copy.24
  544.5 0.2 all-gather.13.cloned.1.call-start
  544.8 3.1 broadcast_multiply_fusion.1
  547.9 0.3 fusion.36
  548.2 131.8 %all-gather.11.cloned.1.call-done = bf16[128,1,4096]{2,1,0:T(2,128)(2,1)} async-done(((bf16[1,1,4096]{2,1,0:T(2,128)(2,1)}), bf16[128,1,4096]{2,1,0:T(2,128)(2,1)}) %all-gather.11.cloned.1.call-update) | async-done | bytes 1048592 | tf_op jit(solution)/shard_map/all_gather | solution.py:47
  680.0 3.1 fusion.1
  683.1 0.3 convolution_bitcast_fusion.1
  683.4 29.2 %all-gather.7.cloned.1.call-done = bf16[128,4,1440]{2,0,1:T(8,128)(2,1)} async-done(((bf16[32,4,1440]{2,0,1:T(8,128)(2,1)}), bf16[128,4,1440]{2,0,1:T(8,128)(2,1)}) %all-gather.7.cloned.1.call-update) | async-done | bytes 1474576 | tf_op jit(solution)/shard_map/all_gather | solution.py:86
  712.6 3.1 fusion.19
  715.7 0.3 convolution_bitcast_fusion.2
  715.9 1.9 fusion.37
  717.8 2.0 convolution_bitcast_fusion.4
  719.8 515.4 %all-reduce.6 = (bf16[128,4096]{1,0:T(8,128)(2,1)}, f32[128,32]{0,1:T(8,128)S(1)}) all-reduce(f32[128,4096]{1,0:T(8,128)S(1)} %fusion.37, f32[128,32]{0,1:T(8,128)S(1)} %convolution_bitcast_fusion.4), channel_id=3, replica_groups=mesh['lat'=128,'ch'=4] {'lat'}, use_global_device_ids=true, to_apply=%region_1.2.clone | all-reduce | flops 528384 | bytes 3178496
  1235.2 1.5 fusion.57
  1236.8 9.0 all_gather.21
  1245.8 0.2 fusion.52
  1246.0 0.1 fusion.51
  1246.1 0.1 fusion.9
  1246.2 0.2 fusion.10
  1246.5 0.1 pad_maximum_fusion.1
  1246.5 0.6 reshape.203
  1247.2 0.5 all-gather.9.cloned.1.call-update
  1247.8 2.0 copy.28
  1249.8 0.2 fusion.55
  1250.0 0.2 fusion.3
  1250.2 0.1 fusion.56
  1250.4 0.2 fusion.4
  1250.6 0.6 maximum_multiply_fusion.2
  1251.2 0.6 broadcast_multiply_fusion.2
  1251.8 130.8 %all-gather.13.cloned.1.call-done = bf16[128,1,4096]{2,1,0:T(2,128)(2,1)} async-done(((bf16[1,1,4096]{2,1,0:T(2,128)(2,1)}), bf16[128,1,4096]{2,1,0:T(2,128)(2,1)}) %all-gather.13.cloned.1.call-update) | async-done | bytes 1048592 | tf_op jit(solution)/shard_map/all_gather | solution.py:47
  1382.7 3.2 fusion.2
  1385.9 0.3 convolution_bitcast_fusion
  1386.1 28.4 %all-gather.9.cloned.1.call-done = bf16[128,4,1440]{2,0,1:T(8,128)(2,1)} async-done(((bf16[32,4,1440]{2,0,1:T(8,128)(2,1)}), bf16[128,4,1440]{2,0,1:T(8,128)(2,1)}) %all-gather.9.cloned.1.call-update) | async-done | bytes 1474576 | tf_op jit(solution)/shard_map/all_gather | solution.py:129
  1414.6 1.8 fusion
  1416.3 1.1 copy.29
  (22 shorter events, 0.3 us)
Async XLA Ops:
  7.2 672.8 %copy-start = (f32[512,128]{1,0:T(8,128)S(1)}, f32[512,128]{1,0:T(8,128)}, u32[]{:S(2)}) copy-start(f32[512,128]{1,0:T(8,128)} %param.8) | copy-start | bytes 786436
  7.2 672.8 %all-gather.11.cloned.1.call-start = ((), (), s32[]{:S(2)}) async-start(), calls=%async_computation.2 | async-start | bytes 2113536 | tf_op jit(solution)/shard_map/all_gather | solution.py:47
  7.2 3.4 copy-start.2
  13.6 528.3 %copy-start.3 = (bf16[1,2,128,128]{3,2,1,0:T(8,128)(2,1)S(1)}, bf16[1,2,128,128]{3,2,1,0:T(8,128)(2,1)}, u32[]{:S(2)}) copy-start(bf16[1,2,128,128]{3,2,1,0:T(8,128)(2,1)} %param.9) | copy-start | bytes 196612
  543.6 169.0 %all-gather.7.cloned.1.call-start = ((), (), s32[]{:S(2)}) async-start(), calls=%async_computation | async-start | bytes 1966080 | tf_op jit(solution)/shard_map/all_gather | solution.py:86
  544.5 838.1 %all-gather.13.cloned.1.call-start = ((), (), s32[]{:S(2)}) async-start(), calls=%async_computation.3 | async-start | bytes 2113536 | tf_op jit(solution)/shard_map/all_gather | solution.py:47
  548.2 164.4 %copy-start.5 = (bf16[128,128]{1,0:T(8,128)(2,1)S(1)}, bf16[128,128]{1,0:T(8,128)(2,1)}, u32[]{:S(2)}) copy-start(bf16[128,128]{1,0:T(8,128)(2,1)} %param.10) | copy-start | bytes 98308
  548.2 164.4 %copy-start.6 = (bf16[32,4,1440]{2,1,0:T(4,128)(2,1)S(1)}, bf16[32,4,1440]{2,1,0:T(4,128)(2,1)}, u32[]{:S(2)}) copy-start(bf16[32,4,1440]{2,1,0:T(4,128)(2,1)} %param.11) | copy-start | bytes 1105924
  715.7 4.1 copy-start.1
  719.8 526.0 %copy-start.4 = (bf16[1,2,128,128]{3,2,1,0:T(8,128)(2,1)S(1)}, bf16[1,2,128,128]{3,2,1,0:T(8,128)(2,1)}, u32[]{:S(2)}) copy-start(bf16[1,2,128,128]{3,2,1,0:T(8,128)(2,1)} %param.9) | copy-start | bytes 196612
  1247.2 167.4 %all-gather.9.cloned.1.call-start = ((), (), s32[]{:S(2)}) async-start(), calls=%async_computation.1 | async-start | bytes 1966080 | tf_op jit(solution)/shard_map/all_gather | solution.py:129
Sparse Core Ops, SparseCore 0:
  543.7 136.1 all-gather.10
  682.6 29.9 all-gather.6
  1247.3 135.2 all-gather.12
  1384.6 29.9 all-gather.8
where the time goes:
time: 1420 us
  blocking collectives  1050 us (74%)
  waiting for transfers between devices  321 us (23%)
  matrix products  21.2 us (1%)
    unnamed x2, blocking collectives  1030 us
    all_gather x2, waiting for transfers between devices, gather_modes(): lax.all_gather(coefficients, 'lat', axis=0, tiled=True).astype(jnp.float32)  263 us
    all_gather x1, waiting for transfers between devices, on_device(): features_all = lax.all_gather(features, 'ch', axis=0, tiled=True)  29.2 us
    all_gather x1, waiting for transfers between devices, on_device(): g_pre_all = lax.all_gather(g_pre, 'ch', axis=0, tiled=True)  28.4 us
  transfers between devices with their start and end apart: 4, of which 4 were waited for; matrix products, arithmetic and copies ran while one was open for 1% of the time, Pallas kernels for 0%

commit v1 on v0

v1 whole, which is shorter than its diff:
```python
import math

import jax
import jax.numpy as jnp
import numpy as np
from jax import lax
from jax.experimental import pallas as pl
from jax.experimental.pallas import tpu as pltpu
from jax.sharding import PartitionSpec as P

MESH = pl.DeviceIdType.MESH
F32 = jnp.float32
BF16 = jnp.bfloat16

M = 64
NLON = 1440
C = 128
X, Y, Z, K = 4, 4, 16, 2
B = Y * K
PLANE = X * B
GROUP = C // X
ROWS = 4
CHUNK = 16


def fourier_table():
    column = np.arange(NLON)
    mode = np.arange(M)
    phase = (mode[:, None] * column[None, :] % NLON) * (2.0 * math.pi / NLON)
    table = np.concatenate([np.cos(phase), -np.sin(phase)], 0) / math.sqrt(NLON)
    return jnp.asarray(table.astype(np.float32), BF16)


def shuffle_table():
    table = np.zeros((ROWS, GROUP, ROWS, ROWS, ROWS, GROUP), np.float32)
    for jj in range(4):
        for c in range(GROUP):
            for a in range(ROWS):
                table[jj, c, a, a, jj, c] = 1
    return jnp.asarray(table.reshape(512, 512), BF16)


def row_table():
    table = np.zeros((Z, X, B, C), np.float32)
    for z in range(Z):
        for b in range(B):
            table[z, :, b, (b // K) * Z * K + z * K + b % K] = 1
    return jnp.asarray(table.reshape(512, C), BF16)


def iota(shape, dim):
    return lax.broadcasted_iota(jnp.int32, shape, dim)


def dot(left, right):
    return jnp.dot(left, right, preferred_element_type=F32)


def dot_t(left, right):
    return lax.dot_general(left, right, (((1,), (1,)), ((), ())), preferred_element_type=F32)


def onehot(mask):
    return jnp.where(mask, 1.0, 0.0).astype(BF16)


def swap_blocks(v):
    lane = iota((8, 128), 1) // 32
    parts = [v[8 * p : 8 * p + 8] for p in range(4)]
    rows = []
    for q in range(4):
        row = parts[q]
        for p in range(4):
            if p != q:
                row = jnp.where(lane == p, pltpu.roll(parts[p], ((p - q) * 32) % 128, 1), row)
        rows.append(row)
    return jnp.concatenate(rows, 0)


def kernel(
    f_ref, cot_ref, p_ref, s_ref, w_ref, skip_ref, tt_ref, shuffle_ref, pick_ref,
    out_ref, gf_ref, gw_ref, gk_ref,
    fall, gall, wall, act, pbig, sbig, pbig_t, sbig_t, kron1, kron2,
    xs, xr, ys, yr, ms, mr, vs, vr,
    bxs, bxr, bys, byr, bms, bmr, bvs, bvr,
    gws, gwr, k1s, k1r, k2s, k2r, k3r,
    send, recv, local,
):
    lat = lax.axis_index("lat")
    x = lax.axis_index("ch")
    y, z, core = lat // (Z * K), (lat // K) % Z, lat % K
    b = y * K + core
    me = x * B + b

    def plane_device(s):
        bb = s % B
        return ((bb // K) * (Z * K) + z * K + bb % K, s // B)

    def z_device(zz):
        return (y * (Z * K) + zz * K + core, x)

    def remote(src, dst, slot, device):
        return pltpu.make_async_remote_copy(
            src_ref=src, dst_ref=dst, send_sem=send.at[slot], recv_sem=recv.at[slot],
            device_id=device, device_id_type=MESH,
        )

    def to_plane(slot, src, dst):
        @pl.loop(1, PLANE)
        def _(i):
            s = lax.rem(me + i, PLANE)
            remote(src.at[s], dst.at[me], slot, plane_device(s)).start()

        dst[me] = src[me]

    def to_column(slot, src, dst, indexed):
        @pl.loop(1, Z)
        def _(i):
            zz = lax.rem(z + i, Z)
            remote(src.at[zz] if indexed else src, dst.at[z], slot, z_device(zz)).start()

        dst[z] = src[z] if indexed else src[...]

    def wait_recv(slot, dst, count):
        part = dst.at[pl.ds(0, count)]
        pltpu.make_async_copy(part, part, recv.at[slot]).wait()

    def wait_send(slot, dst, count):
        part = dst.at[pl.ds(0, count)]
        pltpu.make_async_copy(part, part, send.at[slot]).wait()

    barrier = pltpu.get_barrier_semaphore()

    @pl.loop(1, PLANE)
    def _(i):
        pl.semaphore_signal(
            barrier, inc=1, device_id=plane_device(lax.rem(me + i, PLANE)), device_id_type=MESH
        )

    @pl.loop(1, Z)
    def _(i):
        pl.semaphore_signal(
            barrier, inc=1, device_id=z_device(lax.rem(z + i, Z)), device_id_type=MESH
        )

    def spread(values, dst):
        rounded = values.astype(BF16)
        cat = jnp.concatenate([rounded[32 * jj : 32 * jj + 32] for jj in range(4)], 1)
        for a in range(ROWS):
            dst[:, a, :] = dot(cat, shuffle_ref[:, 128 * a : 128 * a + 128])

    def collect(src):
        cat = jnp.concatenate([src[:, a, :] for a in range(ROWS)], 1).astype(BF16)
        wide = dot_t(cat, shuffle_ref[...])
        tall = jnp.concatenate([wide[:, 128 * jj : 128 * jj + 128] for jj in range(4)], 0)
        return tall.T

    def partial_sums(big, src, dst):
        rows = jnp.concatenate([src[:, a, :] for a in range(ROWS)], 0).astype(BF16)
        dst[...] = dot(big[...], rows).astype(BF16).reshape(Z, 32, 128)

    def total(src):
        acc = src[0].astype(F32)
        for zz in range(1, Z):
            acc = acc + src[zz].astype(F32)
        return swap_blocks(acc)

    def expand_rows(big, src, dst):
        v = dot(big[...], src[...].reshape(512, 128))
        for a in range(ROWS):
            dst[:, a, :] = swap_blocks(v[32 * a : 32 * a + 32])

    def mode_rows(values, mode):
        return jnp.where(iota((32, 128), 0) % 8 == mode, values, 0.0).astype(BF16)

    spread(dot_t(tt_ref[...], f_ref[...]), xs)
    pl.semaphore_wait(barrier, PLANE - 1 + Z - 1)

    to_plane(0, xs, xr)

    def gather_x(slot, src, dst):
        @pl.loop(1, X)
        def _(i):
            remote(src, dst.at[x], slot, (lat, lax.rem(x + i, X))).start()

        dst[x] = src[...]

    @pl.loop(1, B)
    def _(i):
        bb = lax.rem(b + i, B)
        remote(w_ref.at[0], wall.at[b], 1, plane_device(x * B + bb)).start()

    wall[b] = w_ref[0]
    gather_x(2, f_ref, fall)

    row = iota((128, 512), 0)
    bb = row % B
    pick_a = onehot(
        iota((128, 512), 1) == (bb // K) * (Z * K * ROWS) + (z * K + bb % K) * ROWS + row // 32
    )
    p_rows = dot_t(pick_a, p_ref[...].astype(BF16)).astype(BF16)
    s_rows = dot(pick_a, s_ref[...].astype(BF16)).astype(BF16)
    same = (iota((512, 128), 0) // 8) % 4 == (iota((512, 128), 1) // 8) % 4
    same_t = (iota((128, 512), 0) // 8) % 4 == (iota((128, 512), 1) // 8) % 4
    pick = pick_ref[...]
    pbig[...] = jnp.where(same, dot_t(pick, p_rows), 0.0).astype(BF16)
    sbig[...] = jnp.where(same_t, dot_t(s_rows, pick), 0.0).astype(BF16)

    wait_recv(0, xr, PLANE - 1)
    partial_sums(pbig, xr, ys)
    to_column(3, ys, yr, True)

    sbig_t[...] = jnp.where(same, dot_t(pick, s_rows), 0.0).astype(BF16)
    pbig_t[...] = jnp.where(same_t, dot_t(p_rows, pick), 0.0).astype(BF16)
    own = onehot(iota((128, 128), 1) == x * GROUP + iota((128, 128), 0) // ROWS)
    each = onehot(iota((128, 512), 0) == iota((128, 512), 1) // ROWS)
    same_row = iota((128, 512), 0) % ROWS == iota((128, 512), 1) % ROWS
    skip = skip_ref[...]
    kron1[...] = jnp.where(same_row, dot(dot_t(own, skip).astype(BF16), each), 0.0).astype(BF16)
    kron2[...] = jnp.where(same_row, dot(dot(own, skip).astype(BF16), each), 0.0).astype(BF16)

    wait_recv(1, wall, B - 1)
    wait_recv(3, yr, Z - 1)
    spectral = total(yr).astype(BF16).astype(F32)
    w0 = wall[:, 0].reshape(B * C, C)
    w1 = wall[:, 1].reshape(B * C, C)
    wide = jnp.concatenate([mode_rows(spectral, m) for m in range(B)], 1)
    r0, r1 = dot(wide, w0), dot(wide, w1)
    mixed = jnp.concatenate([r0[:16] - r1[16:], r0[16:] + r1[:16]], 0)
    ms[...] = mixed.astype(BF16)
    to_column(4, ms, mr, False)
    for jj in range(4):
        gws[:, jj, :] = spectral[8 * jj : 8 * jj + 8]

    wait_recv(2, fall, X - 1)
    acc = dot(kron1[:, 0:128], fall[0])
    for g in range(1, X):
        acc = acc + dot(kron1[:, 128 * g : 128 * g + 128], fall[g])
    act[...] = acc

    wait_recv(4, mr, Z - 1)
    expand_rows(sbig, mr, vs)
    to_plane(5, vs, vr)

    col = iota((128, 128), 1) % M
    doubling = jnp.where(col == 0, 1.0, 2.0)
    wait_recv(5, vr, PLANE - 1)
    v_modes = (collect(vr) * doubling).astype(BF16)
    act[...] += dot(v_modes, tt_ref[...])

    scale = math.sqrt(2.0 / math.pi)

    g_ref = gall.at[x]

    @pl.loop(0, 128 // CHUNK)
    def _(i):
        rows = pl.ds(pl.multiple_of(i * CHUNK, CHUNK), CHUNK)
        u = act[rows, :]
        square = u * u
        t = jnp.tanh(scale * u * (1.0 + 0.044715 * square))
        cdf = 0.5 * (1.0 + t)
        out_ref[rows, :] = (u * cdf).astype(BF16)
        slope = cdf + 0.5 * u * (1.0 - t * t) * (scale * (1.0 + 3 * 0.044715 * square))
        g_ref[rows, :] = (cot_ref[rows, :].astype(F32) * slope).astype(BF16)

    g_pre = g_ref[...]
    row = iota((128, 128), 0) % M
    doubling_t = jnp.where(row == 0, 1.0, 2.0)
    spread(dot_t(tt_ref[...], g_pre) * doubling_t, bxs)
    to_plane(6, bxs, bxr)

    @pl.loop(1, X)
    def _(i):
        remote(g_ref, gall.at[x], 7, (lat, lax.rem(x + i, X))).start()

    wait_recv(6, bxr, PLANE - 1)
    partial_sums(sbig_t, bxr, bys)
    to_column(8, bys, byr, True)

    same_lane = iota((128, 128), 0) % ROWS == iota((128, 128), 1) % ROWS
    term = jnp.zeros((128, 128), F32)
    for g in range(X):
        full = jnp.where(same_lane, dot_t(g_pre, fall[g]), 0.0)
        lanes = jnp.where(iota((128, 128), 1) == GROUP * g + iota((128, 128), 0) // ROWS, 1.0, 0.0)
        term = term + jnp.dot(
            full, lanes, precision=lax.Precision.HIGHEST, preferred_element_type=F32
        )
    fold = jnp.where(iota((32, 128), 0) == iota((32, 128), 1) // ROWS, 1.0, 0.0)
    term = jnp.dot(fold, term, precision=lax.Precision.HIGHEST, preferred_element_type=F32)
    for i in range(ROWS):
        k1s[:, i, :] = term[8 * i : 8 * i + 8]

    @pl.loop(1, B)
    def _(i):
        bb = lax.rem(b + i, B)
        remote(k1s.at[bb], k1r.at[b], 9, plane_device(x * B + bb)).start()

    k1r[b] = k1s[b]

    wait_recv(8, byr, Z - 1)
    g_mixed = total(byr).astype(BF16).astype(F32)
    r0 = jnp.zeros((32, C), F32)
    r1 = jnp.zeros((32, C), F32)
    for m in range(B):
        masked = mode_rows(g_mixed, m)
        r0 = r0 + dot_t(masked, wall[m, 0])
        r1 = r1 + dot_t(masked, wall[m, 1])
    g_spectral = jnp.concatenate([r0[:16] + r1[16:], r0[16:] - r1[:16]], 0)
    bms[...] = g_spectral.astype(BF16)
    to_column(10, bms, bmr, False)

    for jj in range(4):
        gws[:, 4 + jj, :] = g_mixed[8 * jj : 8 * jj + 8]

    @pl.loop(1, PLANE)
    def _(i):
        s = lax.rem(me + i, PLANE)
        remote(gws.at[s % B], gwr.at[me], 11, plane_device(s)).start()

    gwr[me] = gws[b]

    wait_recv(9, k1r, B - 1)
    acc = k1r[0]
    for i in range(1, B):
        acc = acc + k1r[i]
    k2s[...] = acc

    @pl.loop(1, Z)
    def _(i):
        remote(k2s, k2r.at[z], 12, z_device(lax.rem(z + i, Z))).start()

    k2r[z] = k2s[...]

    wait_recv(10, bmr, Z - 1)
    expand_rows(pbig_t, bmr, bvs)
    to_plane(13, bvs, bvr)

    wait_recv(7, gall, X - 1)
    acc = dot(kron2[:, 0:128], gall[0])
    for g in range(1, X):
        acc = acc + dot(kron2[:, 128 * g : 128 * g + 128], gall[g])
    act[...] = acc

    wait_recv(12, k2r, Z - 1)
    acc = k2r[0]
    for i in range(1, Z):
        acc = acc + k2r[i]
    k3r[b] = acc * (1.0 / math.sqrt(Y * Z * K * ROWS * NLON))

    @pl.loop(1, B)
    def _(i):
        bb = lax.rem(b + i, B)
        remote(k3r.at[b], k3r.at[b], 14, plane_device(x * B + bb)).start()

    wait_recv(11, gwr, PLANE - 1)
    s_all = jnp.concatenate([gwr[:, jj, :] for jj in range(4)], 0).T.astype(BF16)
    g_all = jnp.concatenate([gwr[:, 4 + jj, :] for jj in range(4)], 0).astype(BF16)
    pick_o = onehot(iota((128, GROUP), 0) == x * GROUP + iota((128, GROUP), 1))
    g_own = dot(g_all, pick_o)
    g_turn = jnp.concatenate([g_own[64:], -g_own[:64]], 0)
    gw_ref[0, 0] = dot(s_all, g_own.astype(BF16)) * (1.0 / math.sqrt(2 * M))
    gw_ref[0, 1] = dot(s_all, g_turn.astype(BF16)) * (1.0 / math.sqrt(2 * M))

    wait_recv(13, bvr, PLANE - 1)
    gf_ref[...] = (act[...] + dot(collect(bvr).astype(BF16), tt_ref[...])).astype(BF16)

    wait_recv(14, k3r, B - 1)
    gk = jnp.concatenate([k3r[:, i, :] for i in range(ROWS)], 0)
    gk_ref[...] = gk.T

    wait_send(0, xs, PLANE - 1)
    wait_send(1, wall, B - 1)
    wait_send(2, fall, X - 1)
    wait_send(3, ys, Z - 1)
    wait_send(4, mr, Z - 1)
    wait_send(5, vs, PLANE - 1)
    wait_send(6, bxs, PLANE - 1)
    wait_send(7, gall, X - 1)
    wait_send(8, bys, Z - 1)
    wait_send(9, k1s, B - 1)
    wait_send(10, bmr, Z - 1)
    wait_send(11, gwr, PLANE - 1)
    wait_send(12, k2r, Z - 1)
    wait_send(13, bvs, PLANE - 1)
    wait_send(14, k3r, B - 1)


def on_device(features, projection, synthesis, mode_weights, skip_weights, cotangent):
    vmem = pl.BlockSpec(memory_space=pltpu.VMEM)
    plane = pltpu.VMEM((PLANE, ROWS, 128), F32)
    column = pltpu.VMEM((Z, 32, 128), BF16)
    one = pltpu.VMEM((32, 128), BF16)
    tall = pltpu.VMEM((512, 128), BF16)
    flat = pltpu.VMEM((128, 512), BF16)
    field = pltpu.VMEM((X, GROUP * ROWS, NLON), BF16)
    phases = [plane, plane, column, column, one, column, plane, plane]
    out, grad_features, grad_weights, grad_skip = pl.pallas_call(
        kernel,
        out_shape=(
            jax.ShapeDtypeStruct((GROUP * ROWS, NLON), BF16),
            jax.ShapeDtypeStruct((GROUP * ROWS, NLON), BF16),
            jax.ShapeDtypeStruct((1, 2, C, GROUP), F32),
            jax.ShapeDtypeStruct((C, GROUP), F32),
        ),
        in_specs=[vmem] * 9,
        out_specs=[vmem] * 4,
        scratch_shapes=[
            field,
            field,
            pltpu.VMEM((B, 2, C, C), BF16),
            pltpu.VMEM((GROUP * ROWS, NLON), F32),
            tall, flat, flat, tall, flat, flat,
            *phases,
            *phases,
            pltpu.VMEM((B, 8, 128), F32),
            pltpu.VMEM((PLANE, 8, 128), F32),
            pltpu.VMEM((B, ROWS, 128), F32),
            pltpu.VMEM((B, ROWS, 128), F32),
            pltpu.VMEM((ROWS, 128), F32),
            pltpu.VMEM((Z, ROWS, 128), F32),
            pltpu.VMEM((B, ROWS, 128), F32),
            pltpu.SemaphoreType.DMA((15,)),
            pltpu.SemaphoreType.DMA((15,)),
            pltpu.SemaphoreType.DMA,
        ],
        compiler_params=pltpu.CompilerParams(
            collective_id=0, has_side_effects=True, vmem_limit_bytes=40 * 1024 * 1024
        ),
    )(
        features.reshape(GROUP * ROWS, NLON),
        cotangent.reshape(GROUP * ROWS, NLON),
        projection,
        synthesis,
        mode_weights,
        skip_weights,
        fourier_table(),
        shuffle_table(),
        row_table(),
    )
    shape = features.shape
    return (out.reshape(shape), grad_features.reshape(shape), grad_weights, grad_skip)


def solution(mesh):
    placed = (P("ch", "lat", None), P(), P(), P("lat", None, None, None), P(), P("ch", "lat", None))
    return jax.shard_map(
        on_device,
        mesh=mesh,
        in_specs=placed,
        out_specs=(
            P("ch", "lat", None),
            P("ch", "lat", None),
            P("lat", None, None, "ch"),
            P(None, "ch"),
        ),
        check_vma=False,
    )
```

time: 1420 us -> 105 us (0.07)
  blocking collectives: 1050 us -> 0 us
  waiting for transfers between devices: 321 us -> 0 us
  Pallas kernels: 0 us -> 97.2 us
  matrix products: 21.2 us -> 0 us
    unnamed x2 -> x0, blocking collectives: 1030 us -> none
    all_gather x4 -> x0, waiting for transfers between devices: 320 us -> none  [the longest x2 263 us: gather_modes(): lax.all_gather(coefficients, 'lat', axis=0, tiled=True).astype(jnp.float32)]
    pallas_call x0 -> x1, Pallas kernels: none -> 97.2 us  [on_device(): pl.pallas_call(kernel, out_shape=(jax.ShapeDtypeStruct((GROUP * ROWS, NLO...]
    dot_general x23 -> x0, matrix products: 21.2 us -> none  [the longest x19 10.3 us: product(): return jnp.einsum(form, left, right, preferred_element_type=jnp.float32)]
    all_gather x2 -> x0, blocking collectives: 18.4 us -> none  [the longest x1 9.37 us: on_device(): spectral_all = lax.all_gather(spectral, 'ch', axis=1, tiled=True)]
  transfers between devices with their start and end apart: 4 -> 0, of which waited for: 4 -> 0; matrix products, arithmetic and copies ran while one was open for 1% -> 0% of each run, Pallas kernels for 0% -> 0%
where the time goes in v1:
time: 105 us
  Pallas kernels  97.2 us (93%)
  local copies, waits for them, and re-layouts  7.13 us (7%)
    pallas_call x1, Pallas kernels, on_device(): pl.pallas_call(kernel, out_shape=(jax.ShapeDtypeStruct((GROUP * ROWS, NLO...  97.2 us
    unnamed x16, local copies, waits for them, and re-layouts  2.99 us

profile of v1, /device:TPU:1, one launch (start us, length us, event | category | flops | bytes accessed | tf_op | source)
XLA Modules:
  0.0 105.1 jit_solution(16593856015566819330)
XLA Ops:
  0.6 0.0 copy-start.1
  0.6 0.0 copy-start.3
  0.7 0.0 copy-start.4
  0.7 1.2 %reshape.20.f_ref = bf16[128,1440]{1,0:T(8,128)(2,1)S(1)} reshape(bf16[32,4,1440]{2,1,0:T(4,128)(2,1)} %param.9) | data formatting | bytes 737280 | tf_op jit(solution)/shard_map/reshape | solution.py:430
  1.9 0.0 copy-start
  1.9 0.0 copy-start.2
  1.9 1.2 %reshape.21.cot_ref = bf16[128,1440]{1,0:T(8,128)(2,1)S(1)} reshape(bf16[32,4,1440]{2,1,0:T(4,128)(2,1)} %param.14) | data formatting | bytes 737280 | tf_op jit(solution)/shard_map/reshape | solution.py:431
  3.2 0.0 copy-done.1
  3.2 0.0 copy-done.3
  3.2 0.0 copy-done.4
  3.2 0.0 copy-done
  3.2 0.0 copy-done.2
  3.2 0.0 copy-start.5
  3.2 0.8 copy-done.5
  4.0 0.0 copy-start.6
  4.0 0.8 copy-done.6
  4.8 97.2 %shard_map.120 = (bf16[128,1440]{1,0:T(8,128)(2,1)S(1)}, bf16[128,1440]{1,0:T(8,128)(2,1)S(1)}, f32[1,2,128,32]{3,2,1,0:T(8,128)S(1)}, f32[128,32]{1,0:T(8,128)S(1)}) custom-call(bf16[128,1440]{1,0:T(8,128)(2,1)S(1)} %reshape.20.f_ref, bf16[128,1440]{1,0:T(8,128)(2,1)S(1)} %reshape.21.cot_ref, f32[128,512]{1,0:T(8,128)S(1)} %copy-done.2, ...), custom_call_target="tpu_custom_call" | custom-call | tf_op jit(solution)/shard_map/pallas_call | solution.py:397
  102.0 0.8 reshape.22
  102.9 0.7 copy.16
  103.5 0.7 copy.15
  104.2 0.8 reshape.23
Async XLA Ops:
  0.6 2.5 %copy-start.1 = (bf16[128,1440]{1,0:T(8,128)(2,1)S(1)}, bf16[128,1440]{1,0:T(8,128)(2,1)}, u32[]{:S(2)}) copy-start(bf16[128,1440]{1,0:T(8,128)(2,1)} %constant.6.clone.tt_ref) | copy-start | bytes 1105924
  0.6 2.5 %copy-start.3 = (f32[512,128]{1,0:T(8,128)S(1)}, f32[512,128]{1,0:T(8,128)}, u32[]{:S(2)}) copy-start(f32[512,128]{1,0:T(8,128)} %s_ref.1) | copy-start | bytes 786436
  0.7 2.5 %copy-start.4 = (bf16[512,128]{1,0:T(8,128)(2,1)S(1)}, bf16[512,128]{1,0:T(8,128)(2,1)}, u32[]{:S(2)}) copy-start(bf16[512,128]{1,0:T(8,128)(2,1)} %constant.8.clone.pick_ref) | copy-start | bytes 393220
  1.9 1.3 %copy-start = (bf16[512,512]{1,0:T(8,128)(2,1)S(1)}, bf16[512,512]{1,0:T(8,128)(2,1)}, u32[]{:S(2)}) copy-start(bf16[512,512]{1,0:T(8,128)(2,1)} %constant.7.clone.shuffle_ref) | copy-start | bytes 1572868
  1.9 1.3 %copy-start.2 = (f32[128,512]{1,0:T(8,128)S(1)}, f32[128,512]{1,0:T(8,128)}, u32[]{:S(2)}) copy-start(f32[128,512]{1,0:T(8,128)} %p_ref.1) | copy-start | bytes 786436
  3.2 0.8 copy-start.5
  4.0 0.8 copy-start.6

commit v2 on v1

--- a/solution.py
+++ b/solution.py
@@ -78,13 +78,15 @@
 
 
 def kernel(
-    f_ref, cot_ref, p_ref, s_ref, w_ref, skip_ref, tt_ref, shuffle_ref, pick_ref,
+    f_hbm, cot_hbm, p_hbm, s_hbm, w_hbm, skip_hbm, tt_hbm, shuffle_hbm, pick_hbm,
+    out_hbm, gf_hbm, gw_hbm, gk_hbm,
+    f_in, cot_in, p_ref, s_ref, skip_ref, tt_ref, shuffle_ref, pick_ref,
     out_ref, gf_ref, gw_ref, gk_ref,
     fall, gall, wall, act, pbig, sbig, pbig_t, sbig_t, kron1, kron2,
     xs, xr, ys, yr, ms, mr, vs, vr,
     bxs, bxr, bys, byr, bms, bmr, bvs, bvr,
     gws, gwr, k1s, k1r, k2s, k2r, k3r,
-    send, recv, local,
+    send, recv, local, cot_ref,
 ):
     lat = lax.axis_index("lat")
     x = lax.axis_index("ch")
@@ -113,10 +115,14 @@
 
         dst[me] = src[me]
 
+    def far(i):
+        half = i // 2
+        return jnp.where(i % 2 == 0, Z // 2 + half, Z // 2 - half)
+
     def to_column(slot, src, dst, indexed):
         @pl.loop(1, Z)
         def _(i):
-            zz = lax.rem(z + i, Z)
+            zz = lax.rem(z + far(i), Z)
             remote(src.at[zz] if indexed else src, dst.at[z], slot, z_device(zz)).start()
 
         dst[z] = src[z] if indexed else src[...]
@@ -142,6 +148,22 @@
         pl.semaphore_signal(
             barrier, inc=1, device_id=z_device(lax.rem(z + i, Z)), device_id_type=MESH
         )
+
+    def load(src, dst, slot):
+        copy = pltpu.make_async_copy(src, dst, local.at[slot])
+        copy.start()
+        return copy
+
+    loads = [
+        load(src, dst, i)
+        for i, (src, dst) in enumerate(
+            (
+                (f_hbm, f_in), (tt_hbm, tt_ref), (shuffle_hbm, shuffle_ref), (p_hbm, p_ref),
+                (s_hbm, s_ref), (pick_hbm, pick_ref), (w_hbm.at[0], wall.at[b]),
+                (skip_hbm, skip_ref), (cot_hbm, cot_in),
+            )
+        )
+    ]
 
     def spread(values, dst):
         rounded = values.astype(BF16)
@@ -173,31 +195,47 @@
     def mode_rows(values, mode):
         return jnp.where(iota((32, 128), 0) % 8 == mode, values, 0.0).astype(BF16)
 
-    spread(dot_t(tt_ref[...], f_ref[...]), xs)
+    loads[0].wait()
+    fall[x] = f_in[...].reshape(GROUP * ROWS, NLON)
+    own = fall.at[x]
+    loads[1].wait()
+    x_modes = dot_t(tt_ref[...], own[...])
+    loads[2].wait()
+    spread(x_modes, xs)
+    loads[6].wait()
     pl.semaphore_wait(barrier, PLANE - 1 + Z - 1)
 
     to_plane(0, xs, xr)
 
-    def gather_x(slot, src, dst):
+    @pl.loop(1, B)
+    def _(i):
+        bb = lax.rem(b + i, B)
+        remote(wall.at[b], wall.at[b], 1, plane_device(x * B + bb)).start()
+
+    def gather_x(slot, ref, half):
+        block = ref.at[x, pl.ds(half * 64, 64)]
+
         @pl.loop(1, X)
         def _(i):
-            remote(src, dst.at[x], slot, (lat, lax.rem(x + i, X))).start()
-
-        dst[x] = src[...]
-
-    @pl.loop(1, B)
-    def _(i):
-        bb = lax.rem(b + i, B)
-        remote(w_ref.at[0], wall.at[b], 1, plane_device(x * B + bb)).start()
-
-    wall[b] = w_ref[0]
-    gather_x(2, f_ref, fall)
+            remote(block, block, slot, (lat, lax.rem(x + i, X))).start()
+
+    def wait_gather(slot, ref):
+        part = ref.at[pl.ds(0, X - 1), pl.ds(0, 64)]
+        for k in range(2):
+            pltpu.make_async_copy(part, part, recv.at[slot + k]).wait()
+
+    def wait_gather_sent(slot, ref):
+        part = ref.at[pl.ds(0, X - 1), pl.ds(0, 64)]
+        for k in range(2):
+            pltpu.make_async_copy(part, part, send.at[slot + k]).wait()
 
     row = iota((128, 512), 0)
     bb = row % B
     pick_a = onehot(
         iota((128, 512), 1) == (bb // K) * (Z * K * ROWS) + (z * K + bb % K) * ROWS + row // 32
     )
+    for i in (3, 4, 5):
+        loads[i].wait()
     p_rows = dot_t(pick_a, p_ref[...].astype(BF16)).astype(BF16)
     s_rows = dot(pick_a, s_ref[...].astype(BF16)).astype(BF16)
     same = (iota((512, 128), 0) // 8) % 4 == (iota((512, 128), 1) // 8) % 4
@@ -205,19 +243,24 @@
     pick = pick_ref[...]
     pbig[...] = jnp.where(same, dot_t(pick, p_rows), 0.0).astype(BF16)
     sbig[...] = jnp.where(same_t, dot_t(s_rows, pick), 0.0).astype(BF16)
+    sbig_t[...] = jnp.where(same, dot_t(pick, s_rows), 0.0).astype(BF16)
+    pbig_t[...] = jnp.where(same_t, dot_t(p_rows, pick), 0.0).astype(BF16)
 
     wait_recv(0, xr, PLANE - 1)
     partial_sums(pbig, xr, ys)
     to_column(3, ys, yr, True)
-
-    sbig_t[...] = jnp.where(same, dot_t(pick, s_rows), 0.0).astype(BF16)
-    pbig_t[...] = jnp.where(same_t, dot_t(p_rows, pick), 0.0).astype(BF16)
-    own = onehot(iota((128, 128), 1) == x * GROUP + iota((128, 128), 0) // ROWS)
+    gather_x(15, fall, 0)
+
+    loads[7].wait()
+    pick_g = onehot(iota((128, 128), 1) == x * GROUP + iota((128, 128), 0) // ROWS)
     each = onehot(iota((128, 512), 0) == iota((128, 512), 1) // ROWS)
     same_row = iota((128, 512), 0) % ROWS == iota((128, 512), 1) % ROWS
     skip = skip_ref[...]
-    kron1[...] = jnp.where(same_row, dot(dot_t(own, skip).astype(BF16), each), 0.0).astype(BF16)
-    kron2[...] = jnp.where(same_row, dot(dot(own, skip).astype(BF16), each), 0.0).astype(BF16)
+    kron1[...] = jnp.where(same_row, dot(dot_t(pick_g, skip).astype(BF16), each), 0.0).astype(BF16)
+    kron2[...] = jnp.where(same_row, dot(dot(pick_g, skip).astype(BF16), each), 0.0).astype(BF16)
+
+    loads[8].wait()
+    cot_ref[...] = cot_in[...].reshape(GROUP * ROWS, NLON)
 
     wait_recv(1, wall, B - 1)
     wait_recv(3, yr, Z - 1)
@@ -229,18 +272,19 @@
     mixed = jnp.concatenate([r0[:16] - r1[16:], r0[16:] + r1[:16]], 0)
     ms[...] = mixed.astype(BF16)
     to_column(4, ms, mr, False)
+    gather_x(16, fall, 1)
     for jj in range(4):
         gws[:, jj, :] = spectral[8 * jj : 8 * jj + 8]
 
-    wait_recv(2, fall, X - 1)
+    wait_recv(4, mr, Z - 1)
+    expand_rows(sbig, mr, vs)
+    to_plane(5, vs, vr)
+
+    wait_gather(15, fall)
     acc = dot(kron1[:, 0:128], fall[0])
     for g in range(1, X):
         acc = acc + dot(kron1[:, 128 * g : 128 * g + 128], fall[g])
     act[...] = acc
-
-    wait_recv(4, mr, Z - 1)
-    expand_rows(sbig, mr, vs)
-    to_plane(5, vs, vr)
 
     col = iota((128, 128), 1) % M
     doubling = jnp.where(col == 0, 1.0, 2.0)
@@ -269,13 +313,8 @@
     spread(dot_t(tt_ref[...], g_pre) * doubling_t, bxs)
     to_plane(6, bxs, bxr)
 
-    @pl.loop(1, X)
-    def _(i):
-        remote(g_ref, gall.at[x], 7, (lat, lax.rem(x + i, X))).start()
-
-    wait_recv(6, bxr, PLANE - 1)
-    partial_sums(sbig_t, bxr, bys)
-    to_column(8, bys, byr, True)
+    f_in[...] = out_ref[...].reshape(GROUP, ROWS, NLON)
+    store_out = load(f_in, out_hbm, 0)
 
     same_lane = iota((128, 128), 0) % ROWS == iota((128, 128), 1) % ROWS
     term = jnp.zeros((128, 128), F32)
@@ -297,6 +336,17 @@
 
     k1r[b] = k1s[b]
 
+    wait_recv(6, bxr, PLANE - 1)
+    partial_sums(sbig_t, bxr, bys)
+    to_column(8, bys, byr, True)
+    gather_x(17, gall, 0)
+
+    wait_recv(9, k1r, B - 1)
+    acc = k1r[0]
+    for i in range(1, B):
+        acc = acc + k1r[i]
+    k2s[...] = acc
+
     wait_recv(8, byr, Z - 1)
     g_mixed = total(byr).astype(BF16).astype(F32)
     r0 = jnp.zeros((32, C), F32)
@@ -309,6 +359,13 @@
     bms[...] = g_spectral.astype(BF16)
     to_column(10, bms, bmr, False)
 
+    @pl.loop(1, Z)
+    def _(i):
+        zz = lax.rem(z + far(i), Z)
+        remote(k2s, k2r.at[z], 12, z_device(zz)).start()
+
+    k2r[z] = k2s[...]
+
     for jj in range(4):
         gws[:, 4 + jj, :] = g_mixed[8 * jj : 8 * jj + 8]
 
@@ -318,28 +375,21 @@
         remote(gws.at[s % B], gwr.at[me], 11, plane_device(s)).start()
 
     gwr[me] = gws[b]
-
-    wait_recv(9, k1r, B - 1)
-    acc = k1r[0]
-    for i in range(1, B):
-        acc = acc + k1r[i]
-    k2s[...] = acc
-
-    @pl.loop(1, Z)
-    def _(i):
-        remote(k2s, k2r.at[z], 12, z_device(lax.rem(z + i, Z))).start()
-
-    k2r[z] = k2s[...]
+    gather_x(18, gall, 1)
+
+    wait_recv(11, gwr, PLANE - 1)
+    s_all = jnp.concatenate([gwr[:, jj, :] for jj in range(4)], 0).astype(BF16)
+    g_all = jnp.concatenate([gwr[:, 4 + jj, :] for jj in range(4)], 0).astype(BF16)
+    pick_o = onehot(iota((GROUP, 128), 1) == x * GROUP + iota((GROUP, 128), 0))
+    g_own = dot_t(pick_o, g_all)
+    g_turn = jnp.concatenate([g_own[:, 64:], -g_own[:, :64]], 1)
+    gw_ref[0] = dot(g_own.astype(BF16), s_all) * (1.0 / math.sqrt(2 * M))
+    gw_ref[1] = dot(g_turn.astype(BF16), s_all) * (1.0 / math.sqrt(2 * M))
+    store_gw = load(gw_ref, gw_hbm, 1)
 
     wait_recv(10, bmr, Z - 1)
     expand_rows(pbig_t, bmr, bvs)
     to_plane(13, bvs, bvr)
-
-    wait_recv(7, gall, X - 1)
-    acc = dot(kron2[:, 0:128], gall[0])
-    for g in range(1, X):
-        acc = acc + dot(kron2[:, 128 * g : 128 * g + 128], gall[g])
-    act[...] = acc
 
     wait_recv(12, k2r, Z - 1)
     acc = k2r[0]
@@ -352,30 +402,29 @@
         bb = lax.rem(b + i, B)
         remote(k3r.at[b], k3r.at[b], 14, plane_device(x * B + bb)).start()
 
-    wait_recv(11, gwr, PLANE - 1)
-    s_all = jnp.concatenate([gwr[:, jj, :] for jj in range(4)], 0).T.astype(BF16)
-    g_all = jnp.concatenate([gwr[:, 4 + jj, :] for jj in range(4)], 0).astype(BF16)
-    pick_o = onehot(iota((128, GROUP), 0) == x * GROUP + iota((128, GROUP), 1))
-    g_own = dot(g_all, pick_o)
-    g_turn = jnp.concatenate([g_own[64:], -g_own[:64]], 0)
-    gw_ref[0, 0] = dot(s_all, g_own.astype(BF16)) * (1.0 / math.sqrt(2 * M))
-    gw_ref[0, 1] = dot(s_all, g_turn.astype(BF16)) * (1.0 / math.sqrt(2 * M))
+    wait_gather(17, gall)
+    acc = dot(kron2[:, 0:128], gall[0])
+    for g in range(1, X):
+        acc = acc + dot(kron2[:, 128 * g : 128 * g + 128], gall[g])
+    act[...] = acc
+
+    wait_recv(14, k3r, B - 1)
+    gk_ref[...] = jnp.concatenate([k3r[:, i, :] for i in range(ROWS)], 0)
+    store_gk = load(gk_ref, gk_hbm, 2)
 
     wait_recv(13, bvr, PLANE - 1)
-    gf_ref[...] = (act[...] + dot(collect(bvr).astype(BF16), tt_ref[...])).astype(BF16)
-
-    wait_recv(14, k3r, B - 1)
-    gk = jnp.concatenate([k3r[:, i, :] for i in range(ROWS)], 0)
-    gk_ref[...] = gk.T
+    result = act[...] + dot(collect(bvr).astype(BF16), tt_ref[...])
+    gf_ref[...] = result.reshape(GROUP, ROWS, NLON).astype(BF16)
+    store_gf = load(gf_ref, gf_hbm, 3)
 
     wait_send(0, xs, PLANE - 1)
     wait_send(1, wall, B - 1)
-    wait_send(2, fall, X - 1)
+    wait_gather_sent(15, fall)
     wait_send(3, ys, Z - 1)
     wait_send(4, mr, Z - 1)
     wait_send(5, vs, PLANE - 1)
     wait_send(6, bxs, PLANE - 1)
-    wait_send(7, gall, X - 1)
+    wait_gather_sent(17, gall)
     wait_send(8, bys, Z - 1)
     wait_send(9, k1s, B - 1)
     wait_send(10, bmr, Z - 1)
@@ -383,10 +432,12 @@
     wait_send(12, k2r, Z - 1)
     wait_send(13, bvs, PLANE - 1)
     wait_send(14, k3r, B - 1)
+    for copy in (store_out, store_gw, store_gk, store_gf):
+        copy.wait()
 
 
 def on_device(features, projection, synthesis, mode_weights, skip_weights, cotangent):
-    vmem = pl.BlockSpec(memory_space=pltpu.VMEM)
+    anywhere = pl.BlockSpec(memory_space=pl.ANY)
     plane = pltpu.VMEM((PLANE, ROWS, 128), F32)
     column = pltpu.VMEM((Z, 32, 128), BF16)
     one = pltpu.VMEM((32, 128), BF16)
@@ -397,14 +448,26 @@
     out, grad_features, grad_weights, grad_skip = pl.pallas_call(
         kernel,
         out_shape=(
-            jax.ShapeDtypeStruct((GROUP * ROWS, NLON), BF16),
-            jax.ShapeDtypeStruct((GROUP * ROWS, NLON), BF16),
-            jax.ShapeDtypeStruct((1, 2, C, GROUP), F32),
-            jax.ShapeDtypeStruct((C, GROUP), F32),
+            jax.ShapeDtypeStruct((GROUP, ROWS, NLON), BF16),
+            jax.ShapeDtypeStruct((GROUP, ROWS, NLON), BF16),
+            jax.ShapeDtypeStruct((2, GROUP, C), F32),
+            jax.ShapeDtypeStruct((GROUP, C), F32),
         ),
-        in_specs=[vmem] * 9,
-        out_specs=[vmem] * 4,
+        in_specs=[anywhere] * 9,
+        out_specs=[anywhere] * 4,
         scratch_shapes=[
+            pltpu.VMEM((GROUP, ROWS, NLON), BF16),
+            pltpu.VMEM((GROUP, ROWS, NLON), BF16),
+            pltpu.VMEM((C, 512), F32),
+            pltpu.VMEM((512, C), F32),
+            pltpu.VMEM((C, C), BF16),
+            pltpu.VMEM((C, NLON), BF16),
+            pltpu.VMEM((512, 512), BF16),
+            pltpu.VMEM((512, C), BF16),
+            pltpu.VMEM((GROUP * ROWS, NLON), BF16),
+            pltpu.VMEM((GROUP, ROWS, NLON), BF16),
+            pltpu.VMEM((2, GROUP, C), F32),
+            pltpu.VMEM((GROUP, C), F32),
             field,
             field,
             pltpu.VMEM((B, 2, C, C), BF16),
@@ -419,16 +482,17 @@
             pltpu.VMEM((ROWS, 128), F32),
             pltpu.VMEM((Z, ROWS, 128), F32),
             pltpu.VMEM((B, ROWS, 128), F32),
-            pltpu.SemaphoreType.DMA((15,)),
-            pltpu.SemaphoreType.DMA((15,)),
-            pltpu.SemaphoreType.DMA,
+            pltpu.SemaphoreType.DMA((19,)),
+            pltpu.SemaphoreType.DMA((19,)),
+            pltpu.SemaphoreType.DMA((9,)),
+            pltpu.VMEM((GROUP * ROWS, NLON), BF16),
         ],
         compiler_params=pltpu.CompilerParams(
-            collective_id=0, has_side_effects=True, vmem_limit_bytes=40 * 1024 * 1024
+            collective_id=0, has_side_effects=True, vmem_limit_bytes=56 * 1024 * 1024
         ),
     )(
-        features.reshape(GROUP * ROWS, NLON),
-        cotangent.reshape(GROUP * ROWS, NLON),
+        features,
+        cotangent,
         projection,
         synthesis,
         mode_weights,
@@ -437,8 +501,7 @@
         shuffle_table(),
         row_table(),
     )
-    shape = features.shape
-    return (out.reshape(shape), grad_features.reshape(shape), grad_weights, grad_skip)
+    return (out, grad_features, grad_weights.transpose(0, 2, 1)[None], grad_skip.T)
 
 
 def solution(mesh):

time: 105 us -> 84 us (0.80)
  Pallas kernels: 97.2 us -> 79 us
  local copies, waits for them, and re-layouts: 7.13 us -> 4.02 us
    pallas_call x1, Pallas kernels: 97.2 us -> 79 us  [on_device(): pl.pallas_call(kernel, out_shape=(jax.ShapeDtypeStruct((GROUP, ROWS, NLON...]
    reshape x4 -> x0, local copies, waits for them, and re-layouts: 4.14 us -> none  [the longest x1 1.23 us: on_device(): cotangent.reshape(GROUP * ROWS, NLON)]
    unnamed x16 -> x10, local copies, waits for them, and re-layouts: 2.99 us -> 4.02 us
where the time goes in v2:
time: 84 us; the launch traced here: 83.7 us
  Pallas kernels  79 us (94%)
  local copies, waits for them, and re-layouts  4.02 us (5%)
    pallas_call x1, Pallas kernels, on_device(): pl.pallas_call(kernel, out_shape=(jax.ShapeDtypeStruct((GROUP, ROWS, NLON...  79 us
    unnamed x10, local copies, waits for them, and re-layouts  4.02 us

profile of v2, /device:TPU:1, one launch (start us, length us, event | category | flops | bytes accessed | tf_op | source)
XLA Modules:
  0.0 83.7 jit_solution(10772451927602523509)
XLA Ops:
  0.6 79.0 %shard_map.120 = (bf16[32,4,1440]{2,1,0:T(4,128)(2,1)}, bf16[32,4,1440]{2,1,0:T(4,128)(2,1)}, f32[2,32,128]{2,1,0:T(8,128)}, f32[32,128]{1,0:T(8,128)}) custom-call(bf16[32,4,1440]{2,1,0:T(4,128)(2,1)} %f_hbm.1, bf16[32,4,1440]{2,1,0:T(4,128)(2,1)} %cot_hbm.1, f32[128,512]{1,0:T(8,128)} %p_hbm.1, f32[512,128]{1,0:T(8,128)} %s_hbm.1, ...), custom_call_target="tpu_custom_call" | custom-call | tf_op jit(solution)/shard_map/pallas_call | solution.py:448
  79.7 0.0 copy-start
  79.7 1.9 %copy.17 = bf16[32,4,1440]{2,1,0:T(4,128)(2,1)} copy(bf16[32,4,1440]{2,1,0:T(4,128)(2,1)} %get-tuple-element.16) | data formatting | bytes 737280
  81.6 0.0 copy-done
  81.6 0.0 copy-start.1
  81.6 0.7 copy.18
  82.4 0.0 copy-done.1
  82.4 0.0 copy-start.2
  82.4 0.6 copy.19
  83.0 0.1 copy-done.2
  83.1 0.6 copy.20
Async XLA Ops:
  79.7 1.9 %copy-start = (bf16[32,4,1440]{2,1,0:T(4,128)(2,1)S(1)}, bf16[32,4,1440]{2,1,0:T(4,128)(2,1)}, u32[]{:S(2)}) copy-start(bf16[32,4,1440]{2,1,0:T(4,128)(2,1)} %get-tuple-element.17) | copy-start | bytes 1105924
  81.6 0.8 copy-start.1
  82.4 0.7 copy-start.2

commit v3 on v2

--- a/solution.py
+++ b/solution.py
@@ -86,7 +86,7 @@
     xs, xr, ys, yr, ms, mr, vs, vr,
     bxs, bxr, bys, byr, bms, bmr, bvs, bvr,
     gws, gwr, k1s, k1r, k2s, k2r, k3r,
-    send, recv, local, cot_ref,
+    send, recv, local, cot_ref, wall_t,
 ):
     lat = lax.axis_index("lat")
     x = lax.axis_index("ch")
@@ -107,10 +107,17 @@
             device_id=device, device_id_type=MESH,
         )
 
+    def peer(i):
+        def ring(k):
+            return jnp.where(k == 3, 0, jnp.where(k == 2, 3, 2 - k))
+
+        dx, dy, dc = ring(i // B), ring((i // K) % Y), 1 - i % K
+        return ((x + dx) % X) * B + ((y + dy) % Y) * K + (core + dc) % K
+
     def to_plane(slot, src, dst):
-        @pl.loop(1, PLANE)
+        @pl.loop(0, PLANE - 1, unroll=True)
         def _(i):
-            s = lax.rem(me + i, PLANE)
+            s = peer(i)
             remote(src.at[s], dst.at[me], slot, plane_device(s)).start()
 
         dst[me] = src[me]
@@ -120,7 +127,7 @@
         return jnp.where(i % 2 == 0, Z // 2 + half, Z // 2 - half)
 
     def to_column(slot, src, dst, indexed):
-        @pl.loop(1, Z)
+        @pl.loop(1, Z, unroll=True)
         def _(i):
             zz = lax.rem(z + far(i), Z)
             remote(src.at[zz] if indexed else src, dst.at[z], slot, z_device(zz)).start()
@@ -137,16 +144,16 @@
 
     barrier = pltpu.get_barrier_semaphore()
 
-    @pl.loop(1, PLANE)
+    @pl.loop(1, Z, unroll=True)
     def _(i):
         pl.semaphore_signal(
-            barrier, inc=1, device_id=plane_device(lax.rem(me + i, PLANE)), device_id_type=MESH
+            barrier, inc=1, device_id=z_device(lax.rem(z + far(i), Z)), device_id_type=MESH
         )
 
-    @pl.loop(1, Z)
+    @pl.loop(0, PLANE - 1, unroll=True)
     def _(i):
         pl.semaphore_signal(
-            barrier, inc=1, device_id=z_device(lax.rem(z + i, Z)), device_id_type=MESH
+            barrier, inc=1, device_id=plane_device(peer(i)), device_id_type=MESH
         )
 
     def load(src, dst, slot):
@@ -276,6 +283,10 @@
     for jj in range(4):
         gws[:, jj, :] = spectral[8 * jj : 8 * jj + 8]
 
+    for m in range(B):
+        for part in range(2):
+            wall_t[part, 128 * m : 128 * m + 128] = wall[m, part].T
+
     wait_recv(4, mr, Z - 1)
     expand_rows(sbig, mr, vs)
     to_plane(5, vs, vr)
@@ -349,17 +360,13 @@
 
     wait_recv(8, byr, Z - 1)
     g_mixed = total(byr).astype(BF16).astype(F32)
-    r0 = jnp.zeros((32, C), F32)
-    r1 = jnp.zeros((32, C), F32)
-    for m in range(B):
-        masked = mode_rows(g_mixed, m)
-        r0 = r0 + dot_t(masked, wall[m, 0])
-        r1 = r1 + dot_t(masked, wall[m, 1])
+    wide = jnp.concatenate([mode_rows(g_mixed, m) for m in range(B)], 1)
+    r0, r1 = dot(wide, wall_t[0]), dot(wide, wall_t[1])
     g_spectral = jnp.concatenate([r0[:16] + r1[16:], r0[16:] - r1[:16]], 0)
     bms[...] = g_spectral.astype(BF16)
     to_column(10, bms, bmr, False)
 
-    @pl.loop(1, Z)
+    @pl.loop(1, Z, unroll=True)
     def _(i):
         zz = lax.rem(z + far(i), Z)
         remote(k2s, k2r.at[z], 12, z_device(zz)).start()
@@ -436,6 +443,20 @@
         copy.wait()
 
 
+def copy_out(*refs):
+    sources, targets, held = refs[:4], refs[4:8], refs[8:12]
+    loaded, stored = refs[12:]
+    loads = [pltpu.make_async_copy(sources[i], held[i], loaded.at[i]) for i in range(4)]
+    stores = [pltpu.make_async_copy(held[i], targets[i], stored.at[i]) for i in range(4)]
+    for load in loads:
+        load.start()
+    for load, store in zip(loads, stores):
+        load.wait()
+        store.start()
+    for store in stores:
+        store.wait()
+
+
 def on_device(features, projection, synthesis, mode_weights, skip_weights, cotangent):
     anywhere = pl.BlockSpec(memory_space=pl.ANY)
     plane = pltpu.VMEM((PLANE, ROWS, 128), F32)
@@ -445,14 +466,15 @@
     flat = pltpu.VMEM((128, 512), BF16)
     field = pltpu.VMEM((X, GROUP * ROWS, NLON), BF16)
     phases = [plane, plane, column, column, one, column, plane, plane]
-    out, grad_features, grad_weights, grad_skip = pl.pallas_call(
+    results = (
+        jax.ShapeDtypeStruct((GROUP, ROWS, NLON), BF16),
+        jax.ShapeDtypeStruct((GROUP, ROWS, NLON), BF16),
+        jax.ShapeDtypeStruct((2, GROUP, C), F32),
+        jax.ShapeDtypeStruct((GROUP, C), F32),
+    )
+    kept = pl.pallas_call(
         kernel,
-        out_shape=(
-            jax.ShapeDtypeStruct((GROUP, ROWS, NLON), BF16),
-            jax.ShapeDtypeStruct((GROUP, ROWS, NLON), BF16),
-            jax.ShapeDtypeStruct((2, GROUP, C), F32),
-            jax.ShapeDtypeStruct((GROUP, C), F32),
-        ),
+        out_shape=results,
         in_specs=[anywhere] * 9,
         out_specs=[anywhere] * 4,
         scratch_shapes=[
@@ -486,6 +508,7 @@
             pltpu.SemaphoreType.DMA((19,)),
             pltpu.SemaphoreType.DMA((9,)),
             pltpu.VMEM((GROUP * ROWS, NLON), BF16),
+            pltpu.VMEM((2, B * C, C), BF16),
         ],
         compiler_params=pltpu.CompilerParams(
             collective_id=0, has_side_effects=True, vmem_limit_bytes=56 * 1024 * 1024
@@ -501,6 +524,19 @@
         shuffle_table(),
         row_table(),
     )
+    out, grad_features, grad_weights, grad_skip = pl.pallas_call(
+        copy_out,
+        out_shape=results,
+        in_specs=[anywhere] * 4,
+        out_specs=[anywhere] * 4,
+        scratch_shapes=[
+            *[pltpu.VMEM(r.shape, r.dtype) for r in results],
+            pltpu.SemaphoreType.DMA((4,)),
+            pltpu.SemaphoreType.DMA((4,)),
+        ],
+        compiler_params=pltpu.CompilerParams(vmem_limit_bytes=56 * 1024 * 1024),
+        name="copy_out",
+    )(*kept)
     return (out, grad_features, grad_weights.transpose(0, 2, 1)[None], grad_skip.T)
 
 

time: 84 us -> 79.5 us (0.946)
  local copies, waits for them, and re-layouts: 4.02 us -> 0 us
    unnamed x10 -> x0, local copies, waits for them, and re-layouts: 4.02 us -> none
    pallas_call x1 -> x2, Pallas kernels: 79 us -> 78.7 us  [the longest x1 76.7 us: on_device(): pl.pallas_call(kernel, out_shape=results, in_specs=[anywhere] * 9, out_sp...]
where the time goes in v3:
time: 79.5 us; the launch traced here: 79.3 us
  Pallas kernels  78.7 us (99%)
    pallas_call x1, Pallas kernels, on_device(): pl.pallas_call(kernel, out_shape=results, in_specs=[anywhere] * 9, out_sp...  76.7 us
    pallas_call x1, Pallas kernels, on_device(): pl.pallas_call(copy_out, out_shape=results, in_specs=[anywhere] * 4, out_...  1.94 us

profile of v3, /device:TPU:1, one launch (start us, length us, event | category | flops | bytes accessed | tf_op | source)
XLA Modules:
  0.0 79.3 jit_solution(10240554751662509649)
XLA Ops:
  0.6 76.7 %shard_map.120 = (bf16[32,4,1440]{2,1,0:T(4,128)(2,1)}, bf16[32,4,1440]{2,1,0:T(4,128)(2,1)}, f32[2,32,128]{2,1,0:T(8,128)}, f32[32,128]{1,0:T(8,128)}) custom-call(bf16[32,4,1440]{2,1,0:T(4,128)(2,1)} %f_hbm.1, bf16[32,4,1440]{2,1,0:T(4,128)(2,1)} %cot_hbm.1, f32[128,512]{1,0:T(8,128)} %p_hbm.1, f32[512,128]{1,0:T(8,128)} %s_hbm.1, ...), custom_call_target="tpu_custom_call" | custom-call | tf_op jit(solution)/shard_map/pallas_call | solution.py:475
  77.4 1.9 %copy_out.1 = (bf16[32,4,1440]{2,1,0:T(4,128)(2,1)}, bf16[32,4,1440]{2,1,0:T(4,128)(2,1)}, f32[2,32,128]{2,1,0:T(8,128)}, f32[32,128]{1,0:T(8,128)}) custom-call(bf16[32,4,1440]{2,1,0:T(4,128)(2,1)} %get-tuple-element.12.refs_0_, bf16[32,4,1440]{2,1,0:T(4,128)(2,1)} %get-tuple-element.13.refs_1_, f32[2,32,128]{2,1,0:T(8,128)} %get-tuple-element.14.refs_2_, ...), custom_call_target="tpu_custom_call" | custom-call | tf_op jit(solution)/shard_map/copy_out/pallas_call | solution.py:527

commit v4 on v3

--- a/solution.py
+++ b/solution.py
@@ -86,7 +86,7 @@
     xs, xr, ys, yr, ms, mr, vs, vr,
     bxs, bxr, bys, byr, bms, bmr, bvs, bvr,
     gws, gwr, k1s, k1r, k2s, k2r, k3r,
-    send, recv, local, cot_ref, wall_t,
+    send, recv, local, cot_ref, wall_t, far_sem,
 ):
     lat = lax.axis_index("lat")
     x = lax.axis_index("ch")
@@ -144,11 +144,12 @@
 
     barrier = pltpu.get_barrier_semaphore()
 
-    @pl.loop(1, Z, unroll=True)
-    def _(i):
-        pl.semaphore_signal(
-            barrier, inc=1, device_id=z_device(lax.rem(z + far(i), Z)), device_id_type=MESH
-        )
+    near = Z // 4
+    for i in range(near, 0, -1):
+        for step in (i, Z - i):
+            pl.semaphore_signal(
+                barrier, inc=1, device_id=z_device(lax.rem(z + step, Z)), device_id_type=MESH
+            )
 
     @pl.loop(0, PLANE - 1, unroll=True)
     def _(i):
@@ -161,16 +162,12 @@
         copy.start()
         return copy
 
-    loads = [
-        load(src, dst, i)
-        for i, (src, dst) in enumerate(
-            (
-                (f_hbm, f_in), (tt_hbm, tt_ref), (shuffle_hbm, shuffle_ref), (p_hbm, p_ref),
-                (s_hbm, s_ref), (pick_hbm, pick_ref), (w_hbm.at[0], wall.at[b]),
-                (skip_hbm, skip_ref), (cot_hbm, cot_in),
-            )
-        )
-    ]
+    first = ((f_hbm, f_in), (tt_hbm, tt_ref), (shuffle_hbm, shuffle_ref))
+    rest = (
+        (p_hbm, p_ref), (s_hbm, s_ref), (pick_hbm, pick_ref), (w_hbm.at[0], wall.at[b]),
+        (skip_hbm, skip_ref), (cot_hbm, cot_in),
+    )
+    loads = [load(source, target, i) for i, (source, target) in enumerate(first)]
 
     def spread(values, dst):
         rounded = values.astype(BF16)
@@ -206,11 +203,16 @@
     fall[x] = f_in[...].reshape(GROUP * ROWS, NLON)
     own = fall.at[x]
     loads[1].wait()
+    loads += [load(source, target, 3 + i) for i, (source, target) in enumerate(rest)]
     x_modes = dot_t(tt_ref[...], own[...])
     loads[2].wait()
     spread(x_modes, xs)
     loads[6].wait()
-    pl.semaphore_wait(barrier, PLANE - 1 + Z - 1)
+    pl.semaphore_wait(barrier, PLANE - 1 + 2 * near)
+    for step in (near, Z - near):
+        pl.semaphore_signal(
+            far_sem, inc=1, device_id=z_device(lax.rem(z + step, Z)), device_id_type=MESH
+        )
 
     to_plane(0, xs, xr)
 
@@ -219,22 +221,26 @@
         bb = lax.rem(b + i, B)
         remote(wall.at[b], wall.at[b], 1, plane_device(x * B + bb)).start()
 
-    def gather_x(slot, ref, half):
-        block = ref.at[x, pl.ds(half * 64, 64)]
+    parts = ((0, 32), (32, 48), (80, 48))
+
+    def gather_x(slot, ref, k):
+        block = ref.at[x, pl.ds(*parts[k])]
 
         @pl.loop(1, X)
         def _(i):
-            remote(block, block, slot, (lat, lax.rem(x + i, X))).start()
+            remote(block, block, slot + k, (lat, lax.rem(x + i, X))).start()
 
     def wait_gather(slot, ref):
-        part = ref.at[pl.ds(0, X - 1), pl.ds(0, 64)]
-        for k in range(2):
+        for k in range(3):
+            part = ref.at[pl.ds(0, X - 1), pl.ds(*parts[k])]
             pltpu.make_async_copy(part, part, recv.at[slot + k]).wait()
 
     def wait_gather_sent(slot, ref):
-        part = ref.at[pl.ds(0, X - 1), pl.ds(0, 64)]
-        for k in range(2):
+        for k in range(3):
+            part = ref.at[pl.ds(0, X - 1), pl.ds(*parts[k])]
             pltpu.make_async_copy(part, part, send.at[slot + k]).wait()
+
+    gather_x(15, fall, 0)
 
     row = iota((128, 512), 0)
     bb = row % B
@@ -255,8 +261,9 @@
 
     wait_recv(0, xr, PLANE - 1)
     partial_sums(pbig, xr, ys)
+    pl.semaphore_wait(far_sem, 2)
     to_column(3, ys, yr, True)
-    gather_x(15, fall, 0)
+    gather_x(15, fall, 1)
 
     loads[7].wait()
     pick_g = onehot(iota((128, 128), 1) == x * GROUP + iota((128, 128), 0) // ROWS)
@@ -279,7 +286,7 @@
     mixed = jnp.concatenate([r0[:16] - r1[16:], r0[16:] + r1[:16]], 0)
     ms[...] = mixed.astype(BF16)
     to_column(4, ms, mr, False)
-    gather_x(16, fall, 1)
+    gather_x(15, fall, 2)
     for jj in range(4):
         gws[:, jj, :] = spectral[8 * jj : 8 * jj + 8]
 
@@ -323,6 +330,7 @@
     doubling_t = jnp.where(row == 0, 1.0, 2.0)
     spread(dot_t(tt_ref[...], g_pre) * doubling_t, bxs)
     to_plane(6, bxs, bxr)
+    gather_x(18, gall, 0)
 
     f_in[...] = out_ref[...].reshape(GROUP, ROWS, NLON)
     store_out = load(f_in, out_hbm, 0)
@@ -350,7 +358,7 @@
     wait_recv(6, bxr, PLANE - 1)
     partial_sums(sbig_t, bxr, bys)
     to_column(8, bys, byr, True)
-    gather_x(17, gall, 0)
+    gather_x(18, gall, 1)
 
     wait_recv(9, k1r, B - 1)
     acc = k1r[0]
@@ -382,7 +390,7 @@
         remote(gws.at[s % B], gwr.at[me], 11, plane_device(s)).start()
 
     gwr[me] = gws[b]
-    gather_x(18, gall, 1)
+    gather_x(18, gall, 2)
 
     wait_recv(11, gwr, PLANE - 1)
     s_all = jnp.concatenate([gwr[:, jj, :] for jj in range(4)], 0).astype(BF16)
@@ -409,7 +417,7 @@
         bb = lax.rem(b + i, B)
         remote(k3r.at[b], k3r.at[b], 14, plane_device(x * B + bb)).start()
 
-    wait_gather(17, gall)
+    wait_gather(18, gall)
     acc = dot(kron2[:, 0:128], gall[0])
     for g in range(1, X):
         acc = acc + dot(kron2[:, 128 * g : 128 * g + 128], gall[g])
@@ -420,9 +428,13 @@
     store_gk = load(gk_ref, gk_hbm, 2)
 
     wait_recv(13, bvr, PLANE - 1)
-    result = act[...] + dot(collect(bvr).astype(BF16), tt_ref[...])
-    gf_ref[...] = result.reshape(GROUP, ROWS, NLON).astype(BF16)
-    store_gf = load(gf_ref, gf_hbm, 3)
+    modes = collect(bvr).astype(BF16)
+    stores = [store_out, store_gw, store_gk]
+    for i in range(4):
+        part = act[32 * i : 32 * i + 32] + dot(modes[32 * i : 32 * i + 32], tt_ref[...])
+        held = gf_ref.at[pl.ds(8 * i, 8)]
+        held[...] = part.reshape(8, ROWS, NLON).astype(BF16)
+        stores.append(load(held, gf_hbm.at[pl.ds(8 * i, 8)], 3 + i))
 
     wait_send(0, xs, PLANE - 1)
     wait_send(1, wall, B - 1)
@@ -431,7 +443,7 @@
     wait_send(4, mr, Z - 1)
     wait_send(5, vs, PLANE - 1)
     wait_send(6, bxs, PLANE - 1)
-    wait_gather_sent(17, gall)
+    wait_gather_sent(18, gall)
     wait_send(8, bys, Z - 1)
     wait_send(9, k1s, B - 1)
     wait_send(10, bmr, Z - 1)
@@ -439,7 +451,7 @@
     wait_send(12, k2r, Z - 1)
     wait_send(13, bvs, PLANE - 1)
     wait_send(14, k3r, B - 1)
-    for copy in (store_out, store_gw, store_gk, store_gf):
+    for copy in stores:
         copy.wait()
 
 
@@ -504,11 +516,12 @@
             pltpu.VMEM((ROWS, 128), F32),
             pltpu.VMEM((Z, ROWS, 128), F32),
             pltpu.VMEM((B, ROWS, 128), F32),
-            pltpu.SemaphoreType.DMA((19,)),
-            pltpu.SemaphoreType.DMA((19,)),
+            pltpu.SemaphoreType.DMA((21,)),
+            pltpu.SemaphoreType.DMA((21,)),
             pltpu.SemaphoreType.DMA((9,)),
             pltpu.VMEM((GROUP * ROWS, NLON), BF16),
             pltpu.VMEM((2, B * C, C), BF16),
+            pltpu.SemaphoreType.REGULAR,
         ],
         compiler_params=pltpu.CompilerParams(
             collective_id=0, has_side_effects=True, vmem_limit_bytes=56 * 1024 * 1024

time: 79.5 us -> 78.1 us (0.982)
  Pallas kernels: 78.7 us -> 77.3 us
    pallas_call x1, Pallas kernels: 76.7 us -> 75.4 us  [on_device(): pl.pallas_call(kernel, out_shape=results, in_specs=[anywhere] * 9, out_sp...]
where the time goes in v4:
time: 78.1 us; the launch traced here: 78 us
  Pallas kernels  77.3 us (99%)
    pallas_call x1, Pallas kernels, on_device(): pl.pallas_call(kernel, out_shape=results, in_specs=[anywhere] * 9, out_sp...  75.4 us
    pallas_call x1, Pallas kernels, on_device(): pl.pallas_call(copy_out, out_shape=results, in_specs=[anywhere] * 4, out_...  1.94 us

profile of v4, /device:TPU:1, one launch (start us, length us, event | category | flops | bytes accessed | tf_op | source)
XLA Modules:
  0.0 78.0 jit_solution(13018735343623740032)
XLA Ops:
  0.6 75.4 %shard_map.120 = (bf16[32,4,1440]{2,1,0:T(4,128)(2,1)}, bf16[32,4,1440]{2,1,0:T(4,128)(2,1)}, f32[2,32,128]{2,1,0:T(8,128)}, f32[32,128]{1,0:T(8,128)}) custom-call(bf16[32,4,1440]{2,1,0:T(4,128)(2,1)} %f_hbm.1, bf16[32,4,1440]{2,1,0:T(4,128)(2,1)} %cot_hbm.1, f32[128,512]{1,0:T(8,128)} %p_hbm.1, f32[512,128]{1,0:T(8,128)} %s_hbm.1, ...), custom_call_target="tpu_custom_call" | custom-call | tf_op jit(solution)/shard_map/pallas_call | solution.py:487
  76.0 1.9 %copy_out.1 = (bf16[32,4,1440]{2,1,0:T(4,128)(2,1)}, bf16[32,4,1440]{2,1,0:T(4,128)(2,1)}, f32[2,32,128]{2,1,0:T(8,128)}, f32[32,128]{1,0:T(8,128)}) custom-call(bf16[32,4,1440]{2,1,0:T(4,128)(2,1)} %get-tuple-element.12.refs_0_, bf16[32,4,1440]{2,1,0:T(4,128)(2,1)} %get-tuple-element.13.refs_1_, f32[2,32,128]{2,1,0:T(8,128)} %get-tuple-element.14.refs_2_, ...), custom_call_target="tpu_custom_call" | custom-call | tf_op jit(solution)/shard_map/copy_out/pallas_call | solution.py:540

commit v5 on v4

--- a/solution.py
+++ b/solution.py
@@ -458,8 +458,14 @@
 def copy_out(*refs):
     sources, targets, held = refs[:4], refs[4:8], refs[8:12]
     loaded, stored = refs[12:]
-    loads = [pltpu.make_async_copy(sources[i], held[i], loaded.at[i]) for i in range(4)]
-    stores = [pltpu.make_async_copy(held[i], targets[i], stored.at[i]) for i in range(4)]
+    loads, stores = [], []
+    for i in range(4):
+        step = GROUP // 4
+        for part in [pl.ds(k * step, step) for k in range(4)] if i < 2 else [pl.ds(0, held[i].shape[0])]:
+            n = len(loads)
+            here = held[i].at[part]
+            loads.append(pltpu.make_async_copy(sources[i].at[part], here, loaded.at[n]))
+            stores.append(pltpu.make_async_copy(here, targets[i].at[part], stored.at[n]))
     for load in loads:
         load.start()
     for load, store in zip(loads, stores):
@@ -544,8 +550,8 @@
         out_specs=[anywhere] * 4,
         scratch_shapes=[
             *[pltpu.VMEM(r.shape, r.dtype) for r in results],
-            pltpu.SemaphoreType.DMA((4,)),
-            pltpu.SemaphoreType.DMA((4,)),
+            pltpu.SemaphoreType.DMA((10,)),
+            pltpu.SemaphoreType.DMA((10,)),
         ],
         compiler_params=pltpu.CompilerParams(vmem_limit_bytes=56 * 1024 * 1024),
         name="copy_out",

time: 78.1 us -> 78.3 us (level)
  no operation moved by 1% of the time
where the time goes in v5:
time: 78.3 us; the launch traced here: 78.1 us
  Pallas kernels  77.4 us (99%)
    pallas_call x1, Pallas kernels, on_device(): pl.pallas_call(kernel, out_shape=results, in_specs=[anywhere] * 9, out_sp...  75.4 us
    pallas_call x1, Pallas kernels, on_device(): pl.pallas_call(copy_out, out_shape=results, in_specs=[anywhere] * 4, out_...  2.04 us

profile of v5, /device:TPU:1, one launch (start us, length us, event | category | flops | bytes accessed | tf_op | source)
XLA Modules:
  0.0 78.1 jit_solution(1848306644063403860)
XLA Ops:
  0.6 75.4 %shard_map.120 = (bf16[32,4,1440]{2,1,0:T(4,128)(2,1)}, bf16[32,4,1440]{2,1,0:T(4,128)(2,1)}, f32[2,32,128]{2,1,0:T(8,128)}, f32[32,128]{1,0:T(8,128)}) custom-call(bf16[32,4,1440]{2,1,0:T(4,128)(2,1)} %f_hbm.1, bf16[32,4,1440]{2,1,0:T(4,128)(2,1)} %cot_hbm.1, f32[128,512]{1,0:T(8,128)} %p_hbm.1, f32[512,128]{1,0:T(8,128)} %s_hbm.1, ...), custom_call_target="tpu_custom_call" | custom-call | tf_op jit(solution)/shard_map/pallas_call | solution.py:493
  76.0 2.0 %copy_out.1 = (bf16[32,4,1440]{2,1,0:T(4,128)(2,1)}, bf16[32,4,1440]{2,1,0:T(4,128)(2,1)}, f32[2,32,128]{2,1,0:T(8,128)}, f32[32,128]{1,0:T(8,128)}) custom-call(bf16[32,4,1440]{2,1,0:T(4,128)(2,1)} %get-tuple-element.12.refs_0_, bf16[32,4,1440]{2,1,0:T(4,128)(2,1)} %get-tuple-element.13.refs_1_, f32[2,32,128]{2,1,0:T(8,128)} %get-tuple-element.14.refs_2_, ...), custom_call_target="tpu_custom_call" | custom-call | tf_op jit(solution)/shard_map/copy_out/pallas_call | solution.py:546
